TPU v7x, 32 devices: a whole 2x2x4 slice. The times are simulated.
32 devices in a mesh: dp: 8 (over z, x), tensor: 4 (over y, core).
Axes of the slice: x: 2, y: 2, z: 4, core: 2. Of those that a mesh axis runs over, the one named last changes fastest.
Arguments:
- projections: bfloat16 [3072, 3, 3072], P('dp', None, 'tensor'), may hold values from -5.5 to 5.5
- routes: int32 [3072, 1], replicated, may hold values from 0 to 7; in each aligned block of 384 rows (0 to 383, 384 to 767, ...) at most 64 rows name the same one
- segments: int32 [8, 512], P('dp'), may hold values from 0 to 15, never falling along the last dimension, each value on 1 to 128 neighbouring positions
- out_weight: bfloat16 [3072, 6144], P('tensor'), may hold values from -0.109375 to 0.109375
Outputs:
- attention_out: bfloat16 [3072, 6144], P('dp', 'tensor')
Inputs may be any that keep to these rules, and one draw needn't show every extreme that they name: `routes`: at most 64 of the 384 rows of one device name the same sequence, and in every draw the rows of some device name some sequence exactly 64 times. `segments`: in each row the image numbers never fall, each image covers 1 to 128 positions, and one image covers exactly 128.
All inputs are finite; a program needn't handle non-finite values.
Results may differ from a plain program's by a relative error of at most 0.009.
Values may be sent and summed in bfloat16 or wider, within the bound.
A program may use at most 64 MiB of HBM per device.

v0:
```python
import math

import jax
import jax.numpy as jnp
from jax import lax
from jax.sharding import PartitionSpec as P

HD = 128


def attend_heads(arrived, allowed):
    senders = arrived.shape[0]
    capacity = arrived.shape[1]
    slot_total = senders * capacity
    heads_now = arrived.shape[3]
    head_size = arrived.shape[4]
    flattened = arrived.reshape(slot_total, 3, heads_now, head_size)
    block_rows = min(slot_total, 512)
    block_count = slot_total // block_rows
    queries = flattened[:, 0].reshape(block_count, block_rows, heads_now, head_size)
    mask_rows = allowed.reshape(block_count, block_rows, slot_total)
    keys_in = flattened[:, 1]
    values_in = flattened[:, 2]
    scale = 1.0 / math.sqrt(head_size)

    def one_block(block_pair):
        query_block, mask_block = block_pair
        scores = (
            jnp.einsum("qhd,khd->hqk", query_block, keys_in, preferred_element_type=jnp.float32)
            * scale
        )
        scores = jnp.where(mask_block[None], scores, -jnp.inf)
        highest = jnp.max(scores, axis=2, keepdims=True)
        raised = jnp.exp(scores - highest)
        weights = (raised / jnp.sum(raised, axis=2, keepdims=True)).astype(jnp.bfloat16)
        return jnp.einsum(
            "hqk,khd->qhd", weights, values_in, preferred_element_type=jnp.float32
        ).astype(jnp.bfloat16)

    blocks = lax.map(one_block, (queries, mask_rows))
    return blocks.reshape(senders, capacity, heads_now, head_size)


def local(projections, routes, segments, out_weight):
    senders = lax.axis_size("dp")
    myself = lax.axis_index("dp")
    own_rows = projections.shape[0]
    column_count = projections.shape[2]
    heads_here = column_count // HD
    positions = segments.shape[1]
    capacity = positions // senders
    targets = routes[:, 0]
    my_routes = lax.dynamic_slice_in_dim(targets, myself * own_rows, own_rows)
    sequence_ids = jnp.arange(senders, dtype=jnp.int32)
    one_hot = (my_routes[:, None] == sequence_ids[None, :]).astype(jnp.int32)
    ranking = jnp.sum((jnp.cumsum(one_hot, axis=0) - one_hot) * one_hot, axis=1)
    slot_of_row = my_routes * capacity + ranking
    source_row = (
        jnp.zeros((positions,), jnp.int32)
        .at[slot_of_row]
        .set(jnp.arange(own_rows, dtype=jnp.int32))
    )
    outgoing = projections[source_row].reshape(senders, capacity, 3, heads_here, HD)
    arrivals = jnp.sum((targets.reshape(senders, own_rows) == myself).astype(jnp.int32), axis=1)
    earlier = jnp.cumsum(arrivals) - arrivals
    within = jnp.arange(capacity, dtype=jnp.int32)
    placed = earlier[:, None] + within[None, :]
    filled = within[None, :] < arrivals[:, None]
    flat_index = jnp.arange(positions, dtype=jnp.int32).reshape(senders, capacity)
    image_row = segments[0]
    looked_up = image_row[jnp.minimum(placed, positions - 1)]
    group_ids = jnp.where(filled, looked_up, -1 - flat_index).reshape(positions)
    allowed = group_ids[:, None] == group_ids[None, :]
    attended = attend_heads(
        lax.all_to_all(outgoing, "dp", split_axis=0, concat_axis=0, tiled=True), allowed
    )
    flat_heads = attended.reshape(positions, heads_here * HD)
    partial_value = jnp.dot(flat_heads, out_weight, preferred_element_type=jnp.float32)
    summed = lax.psum_scatter(
        partial_value.astype(jnp.bfloat16), "tensor", scatter_dimension=1, tiled=True
    )
    returned = lax.all_to_all(
        summed.reshape(senders, capacity, summed.shape[1]),
        "dp",
        split_axis=0,
        concat_axis=0,
        tiled=True,
    )
    result = returned.reshape(positions, returned.shape[2])[slot_of_row]
    return result


def solution(mesh):
    in_specs = (P("dp", None, "tensor"), P(), P("dp", None), P("tensor", None))
    out_specs = P("dp", "tensor")
    return jax.shard_map(local, mesh=mesh, in_specs=in_specs, out_specs=out_specs, check_vma=False)
```

profile of v0, /device:TPU:0, one launch (start us, length us, event | category | flops | bytes accessed | tf_op | source)
XLA Modules:
  0.0 217.9 jit_solution(1747461904153777854)
XLA Ops:
  6.5 0.0 copy-start
  6.5 0.8 dynamic-slice_reduce_fusion
  7.4 0.9 reduce-window.18
  8.2 0.2 slice_reduce_fusion
  8.5 0.1 fusion.10
  8.6 0.7 fusion.12
  9.3 2.9 %scatter_custom_fusion = s32[512]{0:T(512)S(1)} fusion(s32[384]{0:T(512)S(1)} %fusion.12, s32[384]{0:T(512)S(1)} %iota.32, s32[]{:T(128)} %constant.19.clone.1), kind=kCustom, calls=%fused_computation.38 | custom fusion | bytes 2052 | tf_op jit(solution)/shard_map/scatter | solution.py:61
  12.3 0.0 copy-done
  12.3 9.0 %gather_fusion = bf16[512,3,768]{2,0,1:T(8,128)(2,1)} fusion(bf16[384,3,768]{2,0,1:T(8,128)(2,1)S(1)} %copy-done, s32[1024]{0:T(1024)S(1)} %pad_clamp_fusion.2), kind=kCustom, calls=%fused_computation | custom fusion | bytes 4720640 | tf_op jit(solution)/shard_map/gather | solution.py:63
  21.3 6.0 %reshape.192 = bf16[8,64,3,6,128]{4,3,1,0,2:T(8,128)(2,1)} reshape(bf16[512,3,768]{2,0,1:T(8,128)(2,1)} %gather_fusion) | data formatting | bytes 4718592 | tf_op jit(solution)/shard_map/reshape | solution.py:63
  27.3 0.0 copy-start.2
  27.3 0.0 copy-start.1
  27.3 4.0 %copy.11 = bf16[8,64,3,6,128]{4,1,3,2,0:T(8,128)(2,1)} copy(bf16[8,64,3,6,128]{4,3,1,0,2:T(8,128)(2,1)} %reshape.192) | data formatting | bytes 4718592 | tf_op jit(solution)/shard_map/reshape | solution.py:63
  31.3 7.3 %all-to-all-start = ((bf16[8,64,3,6,128]{4,1,3,2,0:T(8,128)(2,1)}), bf16[8,64,3,6,128]{4,1,3,2,0:T(8,128)(2,1)}, u32[]{:S(2)}, u32[]{:S(2)}) async-start(bf16[8,64,3,6,128]{4,1,3,2,0:T(8,128)(2,1)} %copy.11), calls=%async_computation | async-start | bytes 4718592 | tf_op jit(solution)/shard_map/all_to_all | solution.py:75
  38.6 0.2 reduce-scatter.2.cloned.1.call-start
  38.8 0.0 copy-done.2
  38.9 0.1 reduce_sum.32
  39.0 0.2 reduce-window.20
  39.2 0.1 compare_select_fusion
  39.3 0.1 reshape.212
  39.3 0.0 copy-done.1
  39.3 3.5 %gather_fusion.1 = s32[512]{0:T(512)S(1)} fusion(s32[512]{0:T(512)S(1)} %bitcast.35, s32[1024]{0:T(1024)S(1)} %pad_clamp_fusion.1), kind=kCustom, calls=%fused_computation.1 | custom fusion | bytes 6144 | tf_op jit(solution)/shard_map/gather | solution.py:71
  42.8 0.1 reshape.211
  42.9 0.1 subtract_select_fusion
  43.0 0.1 select_n.46
  43.1 0.2 broadcast_compare_fusion
  43.3 49.2 %all-to-all-done = bf16[8,64,3,6,128]{4,1,3,2,0:T(8,128)(2,1)} async-done(((bf16[8,64,3,6,128]{4,1,3,2,0:T(8,128)(2,1)}), bf16[8,64,3,6,128]{4,1,3,2,0:T(8,128)(2,1)}, u32[]{:S(2)}, u32[]{:S(2)}) %all-to-all-start) | async-done | bytes 2359328 | tf_op jit(solution)/shard_map/all_to_all | solution.py:75
  92.5 2.2 copy.12
  94.7 1.0 fusion.7
  95.7 0.0 slice-start
  95.7 0.0 slice-start.1
  95.7 3.0 %fusion.17 = (f32[6,512]{1,0:T(8,128)S(1)}, f32[6,512,512]{1,2,0:T(8,128)S(1)}) fusion(f32[6,512,512]{1,2,0:T(8,128)S(1)} %fusion.7, pred[512,512]{0,1:T(8,128)(4,1)S(1)} %broadcast_compare_fusion), kind=kOutput, calls=%fused_computation.44 | output fusion | flops 9437695 | bytes 12857344 | tf_op jit(solution)/shard_map/while/body/eval_jaxpr/sub | solution.py:34
  98.7 0.0 slice-start.2
  98.7 0.8 fusion.6
  99.5 0.0 slice-done
  99.5 0.0 slice-done.1
  99.5 1.4 slice-done.2
  100.9 7.2 %convolution_convert_fusion = bf16[512,6144]{1,0:T(8,128)(2,1)} fusion(bf16[512,768]{0,1:T(8,128)(2,1)S(1)} %bitcast.45, bf16[768,6144]{1,0:T(8,128)(2,1)S(1)} %bitcast.44), kind=kOutput, calls=%fused_computation.5 | convolution fusion | flops 4834983936 | bytes 16515072 | tf_op jit(solution)/shard_map/dot_general | solution.py:78
  108.1 0.0 reduce-scatter.2.cloned.1.call-update
  108.1 57.6 %reduce-scatter.2.cloned.1.call-done = bf16[512,1536]{1,0:T(8,128)(2,1)} async-done(((bf16[512,6144]{1,0:T(8,128)(2,1)}), bf16[512,1536]{1,0:T(8,128)(2,1)}) %reduce-scatter.2.cloned.1.call-update) | async-done | bytes 1572880 | tf_op jit(solution)/shard_map/reduce_scatter | solution.py:79
  165.7 5.5 %all-to-all-start.1 = ((bf16[8,64,1536]{2,1,0:T(8,128)(2,1)}), bf16[8,64,1536]{2,1,0:T(8,128)(2,1)S(1)}, u32[]{:S(2)}, u32[]{:S(2)}) async-start(bf16[8,64,1536]{2,1,0:T(8,128)(2,1)} %bitcast.39), calls=%async_computation.2 | async-start | bytes 3145728 | tf_op jit(solution)/shard_map/all_to_all | solution.py:82
  171.3 37.0 %all-to-all-done.1 = bf16[8,64,1536]{2,1,0:T(8,128)(2,1)S(1)} async-done(((bf16[8,64,1536]{2,1,0:T(8,128)(2,1)}), bf16[8,64,1536]{2,1,0:T(8,128)(2,1)S(1)}, u32[]{:S(2)}, u32[]{:S(2)}) %all-to-all-start.1) | async-done | bytes 1572896 | tf_op jit(solution)/shard_map/all_to_all | solution.py:82
  208.2 2.8 %gather_fusion.2 = bf16[384,1536]{1,0:T(8,128)(2,1)} fusion(bf16[512,1536]{1,0:T(8,128)(2,1)S(1)} %bitcast.36, s32[1024]{0:T(1024)S(1)} %pad_clamp_fusion), kind=kCustom, calls=%fused_computation.2 | custom fusion | bytes 2360832 | tf_op jit(solution)/shard_map/gather | solution.py:89
  (11 shorter events, 0.1 us)
Async XLA Ops:
  6.5 5.7 %copy-start = (bf16[384,3,768]{2,0,1:T(8,128)(2,1)S(1)}, bf16[384,3,768]{2,0,1:T(8,128)(2,1)}, u32[]{:S(2)}) copy-start(bf16[384,3,768]{2,0,1:T(8,128)(2,1)} %param.4) | copy-start | bytes 5308420
  27.3 11.5 %copy-start.2 = (s32[3072,1]{0,1:T(1,128)S(1)}, s32[3072,1]{0,1:T(1,128)}, u32[]{:S(2)}) copy-start(s32[3072,1]{0,1:T(1,128)} %param.5) | copy-start | bytes 36868
  27.3 12.1 %copy-start.1 = (s32[1,512]{1,0:T(1,128)S(1)}, s32[1,512]{1,0:T(1,128)}, u32[]{:S(2)}) copy-start(s32[1,512]{1,0:T(1,128)} %param.6) | copy-start | bytes 6148
  31.3 61.2 %all-to-all-start = ((bf16[8,64,3,6,128]{4,1,3,2,0:T(8,128)(2,1)}), bf16[8,64,3,6,128]{4,1,3,2,0:T(8,128)(2,1)}, u32[]{:S(2)}, u32[]{:S(2)}) async-start(bf16[8,64,3,6,128]{4,1,3,2,0:T(8,128)(2,1)} %copy.11), calls=%async_computation | async-start | bytes 4718592 | tf_op jit(solution)/shard_map/all_to_all | solution.py:75
  38.6 127.2 %reduce-scatter.2.cloned.1.call-start = ((), (), s32[]{:S(2)}) async-start(), calls=%async_computation.3 | async-start | bytes 7864320 | tf_op jit(solution)/shard_map/reduce_scatter | solution.py:79
  95.7 3.8 %slice-start = ((s8[9437184]{0:T(1024)(128)(4,1)}), s8[1048576]{0:T(1024)(128)(4,1)S(1)}, s32[]{:S(2)}) async-start(s8[9437184]{0:T(1024)(128)(4,1)} %bitcast.43), calls=%async_computation.4 | async-start | bytes 2097152
  95.7 3.8 %slice-start.1 = ((s8[9437184]{0:T(1024)(128)(4,1)}), s8[4194304]{0:T(1024)(128)(4,1)S(1)}, s32[]{:S(2)}) async-start(s8[9437184]{0:T(1024)(128)(4,1)} %bitcast.43), calls=%async_computation.5 | async-start | bytes 8388608
  98.7 2.2 %slice-start.2 = ((s8[9437184]{0:T(1024)(128)(4,1)}), s8[4194304]{0:T(1024)(128)(4,1)S(1)}, s32[]{:S(2)}) async-start(s8[9437184]{0:T(1024)(128)(4,1)} %bitcast.43), calls=%async_computation.6 | async-start | bytes 8388608
  165.7 42.5 %all-to-all-start.1 = ((bf16[8,64,1536]{2,1,0:T(8,128)(2,1)}), bf16[8,64,1536]{2,1,0:T(8,128)(2,1)S(1)}, u32[]{:S(2)}, u32[]{:S(2)}) async-start(bf16[8,64,1536]{2,1,0:T(8,128)(2,1)} %bitcast.39), calls=%async_computation.2 | async-start | bytes 3145728 | tf_op jit(solution)/shard_map/all_to_all | solution.py:82
Sparse Core Ops, SparseCore 0:
  108.2 57.4 reduce-scatter.1
where the time goes:
time: 218 us
  waiting for transfers between devices  144 us (66%)
  local copies, waits for them, and re-layouts  33.1 us (15%)
  between operations  13.6 us (6%)
  starting transfers between devices  13 us (6%)
  matrix products  8.94 us (4%)
  other arithmetic  5.45 us (2%)
    reduce_scatter x1, waiting for transfers between devices, local(): lax.psum_scatter(partial_value.astype(jnp.bfloat16), 'tensor', scatter_di...  57.6 us
    all_to_all x1, waiting for transfers between devices, local(): lax.all_to_all(outgoing, 'dp', split_axis=0, concat_axis=0, tiled=True)  49.2 us
    all_to_all x1, waiting for transfers between devices, local(): lax.all_to_all(summed.reshape(senders, capacity, summed.shape[1]), 'dp',...  37 us
    reshape x2, local copies, waits for them, and re-layouts, local(): projections[source_row].reshape(senders, capacity, 3, heads_here, HD)  10 us
    gather x1, local copies, waits for them, and re-layouts, local(): projections[source_row].reshape(senders, capacity, 3, heads_here, HD)  9.03 us
    all_to_all x1, starting transfers between devices, local(): lax.all_to_all(outgoing, 'dp', split_axis=0, concat_axis=0, tiled=True)  7.25 us
    dot_general x1, matrix products, local(): jnp.dot(flat_heads, out_weight, preferred_element_type=jnp.float32)  7.2 us
    all_to_all x1, starting transfers between devices, local(): lax.all_to_all(summed.reshape(senders, capacity, summed.shape[1]), 'dp',...  5.51 us
  transfers between devices with their start and end apart: 3, of which 3 were waited for; matrix products, arithmetic and copies ran while one was open for 2% of the time, Pallas kernels for 0%

commit v1 on v0

v1 whole, which is shorter than its diff:
```python
import functools
import math

import jax
import jax.numpy as jnp
from jax import lax
from jax.experimental import pallas as pl
from jax.experimental.pallas import tpu as pltpu
from jax.sharding import PartitionSpec as P

HD = 128


def routing(routes, segments, own_rows, senders, capacity):
    positions = senders * capacity
    myself = lax.axis_index("dp")
    targets = routes[:, 0]
    mine = lax.dynamic_slice_in_dim(targets, myself * own_rows, own_rows)
    row = jnp.arange(own_rows, dtype=jnp.int32)
    same_before = (mine[:, None] == mine[None, :]) & (row[None, :] < row[:, None])
    slot_of_row = mine * capacity + jnp.sum(same_before.astype(jnp.int32), axis=1)
    arrivals = jnp.sum((targets.reshape(senders, own_rows) == myself).astype(jnp.int32), axis=1)
    device = jnp.arange(senders, dtype=jnp.int32)
    earlier = jnp.sum(jnp.where(device[None, :] < device[:, None], arrivals[None, :], 0), axis=1)
    within = jnp.arange(capacity, dtype=jnp.int32)
    placed = (earlier[:, None] + within[None, :]).reshape(positions)
    filled = (within[None, :] < arrivals[:, None]).reshape(positions)
    flat = jnp.arange(positions, dtype=jnp.int32)
    looked_up = jnp.sum(jnp.where(placed[:, None] == flat[None, :], segments[0][None, :], 0), axis=1)
    return slot_of_row, jnp.where(filled, looked_up, -1 - flat)


def attend_heads(arrived, group_ids):
    slot_total, _, heads_now, head_size = arrived.shape
    block_rows = min(slot_total, 512)
    block_count = slot_total // block_rows
    queries = arrived[:, 0].reshape(block_count, block_rows, heads_now, head_size)
    query_ids = group_ids.reshape(block_count, block_rows)
    keys_in, values_in = arrived[:, 1], arrived[:, 2]
    scale = 1.0 / math.sqrt(head_size)

    def one_block(block_pair):
        query_block, ids = block_pair
        scores = jnp.einsum("qhd,khd->hqk", query_block, keys_in, preferred_element_type=jnp.float32) * scale
        scores = jnp.where((ids[:, None] == group_ids[None, :])[None], scores, -jnp.inf)
        raised = jnp.exp(scores - jnp.max(scores, axis=2, keepdims=True))
        weights = (raised / jnp.sum(raised, axis=2, keepdims=True)).astype(jnp.bfloat16)
        return jnp.einsum("hqk,khd->qhd", weights, values_in, preferred_element_type=jnp.float32).astype(jnp.bfloat16)

    return lax.map(one_block, (queries, query_ids)).reshape(slot_total, heads_now * head_size)


def local(projections, routes, segments, out_weight):
    senders = lax.axis_size("dp")
    own_rows, _, columns = projections.shape
    heads_here = columns // HD
    positions = segments.shape[1]
    capacity = positions // senders
    slot_of_row, group_ids = routing(routes, segments, own_rows, senders, capacity)
    source_row = jnp.zeros((positions,), jnp.int32).at[slot_of_row].set(jnp.arange(own_rows, dtype=jnp.int32))
    outgoing = projections[source_row].reshape(senders, capacity, 3, heads_here, HD)
    arrived = lax.all_to_all(outgoing, "dp", split_axis=0, concat_axis=0, tiled=True)
    attended = attend_heads(arrived.reshape(positions, 3, heads_here, HD), group_ids)
    returned = lax.all_to_all(
        attended.reshape(senders, capacity, columns), "dp", split_axis=0, concat_axis=0, tiled=True
    )
    own = returned.reshape(positions, columns)[slot_of_row]
    partial_value = jnp.dot(own, out_weight, preferred_element_type=jnp.float32)
    return lax.psum_scatter(partial_value.astype(jnp.bfloat16), "tensor", scatter_dimension=1, tiled=True)


def solution(mesh):
    in_specs = (P("dp", None, "tensor"), P(), P("dp", None), P("tensor", None))
    out_specs = P("dp", "tensor")
    return jax.shard_map(local, mesh=mesh, in_specs=in_specs, out_specs=out_specs, check_vma=False)
```

time: 218 us -> 192 us (0.88)
  waiting for transfers between devices: 144 us -> 120 us
  matrix products: 8.94 us -> 11.7 us
  local copies, waits for them, and re-layouts: 33.1 us -> 30.7 us
    all_to_all x1, waiting for transfers between devices: 37 us -> 20.1 us  [local(): lax.all_to_all(attended.reshape(senders, capacity, columns), 'dp', split_...]
    reduce_scatter x1, waiting for transfers between devices: 57.6 us -> 47 us  [local(): lax.psum_scatter(partial_value.astype(jnp.bfloat16), 'tensor', scatter_di...]
    gather x3 -> x1, local copies, waits for them, and re-layouts: 6.36 us -> 2.15 us  [local(): own = returned.reshape(positions, columns)[slot_of_row]]
    all_to_all x1, waiting for transfers between devices: 49.2 us -> 52.9 us  [local(): lax.all_to_all(outgoing, 'dp', split_axis=0, concat_axis=0, tiled=True)]
  transfers between devices with their start and end apart: 3 -> 3, of which waited for: 3 -> 3; matrix products, arithmetic and copies ran while one was open for 2% -> 1% of each run, Pallas kernels for 0% -> 0%
where the time goes in v1:
time: 192 us
  waiting for transfers between devices  120 us (62%)
  local copies, waits for them, and re-layouts  30.7 us (16%)
  between operations  13.5 us (7%)
  matrix products  11.7 us (6%)
  starting transfers between devices  11.1 us (6%)
  other arithmetic  4.85 us (3%)
    all_to_all x1, waiting for transfers between devices, local(): lax.all_to_all(outgoing, 'dp', split_axis=0, concat_axis=0, tiled=True)  52.9 us
    reduce_scatter x1, waiting for transfers between devices, local(): lax.psum_scatter(partial_value.astype(jnp.bfloat16), 'tensor', scatter_di...  47 us
    all_to_all x1, waiting for transfers between devices, local(): lax.all_to_all(attended.reshape(senders, capacity, columns), 'dp', split_...  20.1 us
    reshape x2, local copies, waits for them, and re-layouts, local(): projections[source_row].reshape(senders, capacity, 3, heads_here, HD)  10 us
    dot_general x1, matrix products, local(): partial_value = jnp.dot(own, out_weight, preferred_element_type=jnp.float32)  9.13 us
    gather x1, local copies, waits for them, and re-layouts, local(): projections[source_row].reshape(senders, capacity, 3, heads_here, HD)  9.03 us
    all_to_all x1, starting transfers between devices, local(): lax.all_to_all(outgoing, 'dp', split_axis=0, concat_axis=0, tiled=True)  7.25 us
  transfers between devices with their start and end apart: 3, of which 3 were waited for; matrix products, arithmetic and copies ran while one was open for 1% of the time, Pallas kernels for 0%

profile of v1, /device:TPU:0, one launch (start us, length us, event | category | flops | bytes accessed | tf_op | source)
XLA Modules:
  0.0 191.9 jit_solution(12701144909324972253)
XLA Ops:
  6.5 0.0 copy-start
  6.5 0.8 dynamic-slice_reduce_fusion
  7.4 0.2 convert_reduce_fusion
  7.6 0.7 fusion.11
  8.3 2.9 %scatter_custom_fusion = s32[512]{0:T(512)S(1)} fusion(s32[384]{0:T(512)S(1)} %fusion.11, s32[384]{0:T(512)S(1)} %iota.30, s32[]{:T(128)} %constant.11.clone.1), kind=kCustom, calls=%fused_computation.37 | custom fusion | bytes 2052 | tf_op jit(solution)/shard_map/scatter | solution.py:60
  11.3 0.0 copy-done
  11.3 9.0 %gather_fusion = bf16[512,3,768]{2,0,1:T(8,128)(2,1)} fusion(bf16[384,3,768]{2,0,1:T(8,128)(2,1)S(1)} %copy-done, s32[1024]{0:T(1024)S(1)} %pad_clamp_fusion.1), kind=kCustom, calls=%fused_computation | custom fusion | bytes 4720640 | tf_op jit(solution)/shard_map/gather | solution.py:61
  20.3 6.0 %reshape.89 = bf16[8,64,3,6,128]{4,3,1,0,2:T(8,128)(2,1)} reshape(bf16[512,3,768]{2,0,1:T(8,128)(2,1)} %gather_fusion) | data formatting | bytes 4718592 | tf_op jit(solution)/shard_map/reshape | solution.py:61
  26.3 0.0 copy-start.1
  26.3 0.0 copy-start.2
  26.3 4.0 %copy.18 = bf16[8,64,3,6,128]{4,1,3,2,0:T(8,128)(2,1)} copy(bf16[8,64,3,6,128]{4,3,1,0,2:T(8,128)(2,1)} %reshape.89) | data formatting | bytes 4718592 | tf_op jit(solution)/shard_map/reshape | solution.py:61
  30.3 7.3 %all-to-all-start = ((bf16[8,64,3,6,128]{4,1,3,2,0:T(8,128)(2,1)}), bf16[8,64,3,6,128]{4,1,3,2,0:T(8,128)(2,1)}, u32[]{:S(2)}, u32[]{:S(2)}) async-start(bf16[8,64,3,6,128]{4,1,3,2,0:T(8,128)(2,1)} %copy.18), calls=%async_computation | async-start | bytes 4718592 | tf_op jit(solution)/shard_map/all_to_all | solution.py:62
  37.6 0.0 copy-done.1
  37.6 0.1 reduce_sum.50
  37.8 0.1 select_reduce_fusion.1
  37.9 0.1 iota_add_fusion
  38.0 0.1 add.47
  38.0 0.1 iota_compare_fusion.3
  38.1 0.1 lt.70
  38.2 0.0 copy-done.2
  38.2 0.3 select_reduce_fusion
  38.5 0.2 broadcast_compare_fusion
  38.7 52.9 %all-to-all-done = bf16[8,64,3,6,128]{4,1,3,2,0:T(8,128)(2,1)} async-done(((bf16[8,64,3,6,128]{4,1,3,2,0:T(8,128)(2,1)}), bf16[8,64,3,6,128]{4,1,3,2,0:T(8,128)(2,1)}, u32[]{:S(2)}, u32[]{:S(2)}) %all-to-all-start) | async-done | bytes 2359328 | tf_op jit(solution)/shard_map/all_to_all | solution.py:62
  91.5 2.2 %copy.19 = bf16[8,64,3,6,128]{4,1,0,3,2:T(8,128)(2,1)S(1)} copy(bf16[8,64,3,6,128]{4,1,3,2,0:T(8,128)(2,1)} %all-to-all-done) | data formatting | bytes 4718592 | tf_op jit(solution)/shard_map/all_to_all | solution.py:62
  93.7 1.0 fusion.8
  94.7 3.0 %fusion.16 = (f32[6,512]{1,0:T(8,128)S(1)}, f32[6,512,512]{1,2,0:T(8,128)S(1)}) fusion(f32[6,512,512]{1,2,0:T(8,128)S(1)} %fusion.8, pred[512,512]{0,1:T(8,128)(4,1)S(1)} %broadcast_compare_fusion), kind=kOutput, calls=%fused_computation.42 | output fusion | flops 9437695 | bytes 12857344 | tf_op jit(solution)/shard_map/while/body/eval_jaxpr/sub | solution.py:46
  97.7 1.6 fusion.7
  99.3 1.7 copy.22
  101.0 1.8 reshape_reshape.3
  102.8 3.6 %all-to-all-start.1 = ((bf16[8,64,768]{2,1,0:T(8,128)(2,1)}), bf16[8,64,768]{2,1,0:T(8,128)(2,1)S(1)}, u32[]{:S(2)}, u32[]{:S(2)}) async-start(bf16[8,64,768]{2,1,0:T(8,128)(2,1)} %reshape_reshape.3), calls=%async_computation.1 | async-start | bytes 1572864 | tf_op jit(solution)/shard_map/all_to_all | solution.py:64
  106.4 0.2 reduce-scatter.2.cloned.1.call-start
  106.7 20.1 %all-to-all-done.1 = bf16[8,64,768]{2,1,0:T(8,128)(2,1)S(1)} async-done(((bf16[8,64,768]{2,1,0:T(8,128)(2,1)}), bf16[8,64,768]{2,1,0:T(8,128)(2,1)S(1)}, u32[]{:S(2)}, u32[]{:S(2)}) %all-to-all-start.1) | async-done | bytes 786464 | tf_op jit(solution)/shard_map/all_to_all | solution.py:64
  126.8 2.2 %gather_fusion.1 = bf16[384,768]{1,0:T(8,128)(2,1)S(1)} fusion(bf16[512,768]{1,0:T(8,128)(2,1)S(1)} %bitcast.18, s32[1024]{0:T(1024)S(1)} %pad_clamp_fusion), kind=kCustom, calls=%fused_computation.1 | custom fusion | bytes 1181184 | tf_op jit(solution)/shard_map/gather | solution.py:67
  129.0 9.1 %convolution_convert_fusion = bf16[384,6144]{1,0:T(8,128)(2,1)} fusion(bf16[384,768]{1,0:T(8,128)(2,1)S(1)} %gather_fusion.1, bf16[768,6144]{1,0:T(8,128)(2,1)} %param.7), kind=kOutput, calls=%fused_computation.4 | convolution fusion | flops 3626237952 | bytes 14745600 | tf_op jit(solution)/shard_map/dot_general | solution.py:68
  138.1 0.0 reduce-scatter.2.cloned.1.call-update
  138.1 47.0 %reduce-scatter.2.cloned.1.call-done = bf16[384,1536]{1,0:T(8,128)(2,1)} async-done(((bf16[384,6144]{1,0:T(8,128)(2,1)}), bf16[384,1536]{1,0:T(8,128)(2,1)}) %reduce-scatter.2.cloned.1.call-update) | async-done | bytes 1179664 | tf_op jit(solution)/shard_map/reduce_scatter | solution.py:69
  (7 shorter events, 0.1 us)
Async XLA Ops:
  6.5 4.7 %copy-start = (bf16[384,3,768]{2,0,1:T(8,128)(2,1)S(1)}, bf16[384,3,768]{2,0,1:T(8,128)(2,1)}, u32[]{:S(2)}) copy-start(bf16[384,3,768]{2,0,1:T(8,128)(2,1)} %param.4) | copy-start | bytes 5308420
  26.3 11.3 %copy-start.1 = (s32[3072,1]{0,1:T(1,128)S(1)}, s32[3072,1]{0,1:T(1,128)}, u32[]{:S(2)}) copy-start(s32[3072,1]{0,1:T(1,128)} %param.5) | copy-start | bytes 36868
  26.3 11.9 %copy-start.2 = (s32[1,512]{1,0:T(1,128)S(1)}, s32[1,512]{1,0:T(1,128)}, u32[]{:S(2)}) copy-start(s32[1,512]{1,0:T(1,128)} %param.6) | copy-start | bytes 6148
  30.3 61.2 %all-to-all-start = ((bf16[8,64,3,6,128]{4,1,3,2,0:T(8,128)(2,1)}), bf16[8,64,3,6,128]{4,1,3,2,0:T(8,128)(2,1)}, u32[]{:S(2)}, u32[]{:S(2)}) async-start(bf16[8,64,3,6,128]{4,1,3,2,0:T(8,128)(2,1)} %copy.18), calls=%async_computation | async-start | bytes 4718592 | tf_op jit(solution)/shard_map/all_to_all | solution.py:62
  102.8 24.0 %all-to-all-start.1 = ((bf16[8,64,768]{2,1,0:T(8,128)(2,1)}), bf16[8,64,768]{2,1,0:T(8,128)(2,1)S(1)}, u32[]{:S(2)}, u32[]{:S(2)}) async-start(bf16[8,64,768]{2,1,0:T(8,128)(2,1)} %reshape_reshape.3), calls=%async_computation.1 | async-start | bytes 1572864 | tf_op jit(solution)/shard_map/all_to_all | solution.py:64
  106.4 78.7 %reduce-scatter.2.cloned.1.call-start = ((), (), s32[]{:S(2)}) async-start(), calls=%async_computation.3 | async-start | bytes 5898240 | tf_op jit(solution)/shard_map/reduce_scatter | solution.py:69
Sparse Core Ops, SparseCore 0:
  138.2 46.8 reduce-scatter.1

commit v2 on v1

--- a/solution.py
+++ b/solution.py
@@ -69,7 +69,235 @@
     return lax.psum_scatter(partial_value.astype(jnp.bfloat16), "tensor", scatter_dimension=1, tiled=True)
 
 
+def xor(index, mask, size):
+    result, bit = 0, 1
+    while bit < size:
+        digit = (index // bit) % 2
+        result = result + ((1 - digit) if (mask // bit) % 2 else digit) * bit
+        bit *= 2
+    return result
+
+
+def fused_kernel(
+    senders, heads_step,
+    slot_row_ref, slot_col_ref, ids_row_ref, ids_col_ref, proj_ref, weight_hbm,
+    out_ref,
+    weight, packed, arrived, attended, returned, own, pair_out, pair_in, far_out, far_in, kept,
+    weight_sem, there_send, there_recv, back_send, back_recv, pair_send, pair_recv, far_send, far_recv,
+):
+    own_rows, columns = proj_ref.shape[1], proj_ref.shape[2]
+    chunks, positions, _ = packed.shape
+    capacity = positions // senders
+    width = heads_step * HD
+    block = out_ref.shape[1]
+    pieces, tile = far_out.shape[0], far_out.shape[2]
+    me = lax.axis_index("dp")
+    rank = lax.axis_index("tensor")
+    pair = (rank // 2) * 2 + (1 - rank % 2)
+    far = (1 - rank // 2) * 2 + rank % 2
+    masks = list(range(senders // 2, senders)) + list(range(senders // 2 - 1, 0, -1))
+
+    fetch = pltpu.make_async_copy(weight_hbm, weight, weight_sem)
+    fetch.start()
+    barrier = pltpu.get_barrier_semaphore()
+    for mask in masks:
+        pl.semaphore_signal(barrier, inc=1, device_id=(xor(me, mask, senders), rank), device_id_type=pl.DeviceIdType.MESH)
+    for other in (pair, far):
+        pl.semaphore_signal(barrier, inc=1, device_id=(me, other), device_id_type=pl.DeviceIdType.MESH)
+    pl.semaphore_wait(barrier, len(masks) + 2)
+
+    def rows_of(device):
+        return pl.ds(pl.multiple_of(device * capacity, capacity), capacity)
+
+    def exchange(source, target, send_sem, recv_sem, chunk, mask):
+        peer = xor(me, mask, senders)
+        return pltpu.make_async_remote_copy(
+            src_ref=source.at[chunk, rows_of(peer)],
+            dst_ref=target.at[chunk, rows_of(me)],
+            send_sem=send_sem.at[chunk, mask],
+            recv_sem=recv_sem.at[chunk, mask],
+            device_id=(peer, rank),
+            device_id_type=pl.DeviceIdType.MESH,
+        )
+
+    def arrival(source, target, send_sem, recv_sem, chunk, mask):
+        peer = xor(me, mask, senders)
+        return pltpu.make_async_remote_copy(
+            src_ref=source.at[chunk, rows_of(me)],
+            dst_ref=target.at[chunk, rows_of(peer)],
+            send_sem=send_sem.at[chunk, mask],
+            recv_sem=recv_sem.at[chunk, mask],
+            device_id=(peer, rank),
+            device_id_type=pl.DeviceIdType.MESH,
+        )
+
+    there = (packed, arrived, there_send, there_recv)
+    back = (attended, returned, back_send, back_recv)
+
+    place = lax.broadcasted_iota(jnp.int32, (positions, own_rows), 0) == slot_row_ref[...]
+    place = place.astype(jnp.float32).astype(jnp.bfloat16)
+    for chunk in range(chunks):
+        for part in range(3):
+            piece = proj_ref[part, :, chunk * width:(chunk + 1) * width]
+            packed[chunk, :, part * width:(part + 1) * width] = jnp.dot(
+                place, piece, preferred_element_type=jnp.float32
+            ).astype(jnp.bfloat16)
+        for mask in masks:
+            exchange(*there, chunk, mask).start()
+        arrived[chunk, rows_of(me)] = packed[chunk, rows_of(me)]
+
+    scale = 1.0 / math.sqrt(HD)
+    for chunk in range(chunks):
+        for mask in masks:
+            arrival(*there, chunk, mask).wait_recv()
+        for head in range(heads_step):
+            at = head * HD
+            query = arrived[chunk, :, at:at + HD]
+            key = arrived[chunk, :, width + at:width + at + HD]
+            value = arrived[chunk, :, 2 * width + at:2 * width + at + HD]
+            scores = lax.dot_general(query, key, (((1,), (1,)), ((), ())), preferred_element_type=jnp.float32) * scale
+            scores = jnp.where(ids_col_ref[...] == ids_row_ref[...], scores, -jnp.inf)
+            raised = jnp.exp(scores - jnp.max(scores, axis=1, keepdims=True))
+            weights = (raised / jnp.sum(raised, axis=1, keepdims=True)).astype(jnp.bfloat16)
+            attended[chunk, :, at:at + HD] = jnp.dot(
+                weights, value, preferred_element_type=jnp.float32
+            ).astype(jnp.bfloat16)
+        for mask in masks:
+            exchange(*back, chunk, mask).start()
+        returned[chunk, rows_of(me)] = attended[chunk, rows_of(me)]
+
+    unplace = slot_col_ref[...] == lax.broadcasted_iota(jnp.int32, (own_rows, positions), 1)
+    unplace = unplace.astype(jnp.float32).astype(jnp.bfloat16)
+    for chunk in range(chunks):
+        for mask in masks:
+            arrival(*back, chunk, mask).wait_recv()
+        own[:, chunk * width:(chunk + 1) * width] = jnp.dot(
+            unplace, returned[chunk], preferred_element_type=jnp.float32
+        ).astype(jnp.bfloat16)
+
+    fetch.wait()
+
+    def product(target, piece):
+        start = pl.multiple_of(target * block + piece * tile, tile)
+        return jnp.dot(own[...], weight[:, pl.ds(start, tile)], preferred_element_type=jnp.float32)
+
+    def to_pair(side, piece):
+        return pltpu.make_async_remote_copy(
+            src_ref=pair_out.at[side, piece],
+            dst_ref=pair_in.at[side, piece],
+            send_sem=pair_send.at[side, piece],
+            recv_sem=pair_recv.at[side, piece],
+            device_id=(me, pair),
+            device_id_type=pl.DeviceIdType.MESH,
+        )
+
+    def to_far(piece):
+        return pltpu.make_async_remote_copy(
+            src_ref=far_out.at[piece],
+            dst_ref=far_in.at[piece],
+            send_sem=far_send.at[piece],
+            recv_sem=far_recv.at[piece],
+            device_id=(me, far),
+            device_id_type=pl.DeviceIdType.MESH,
+        )
+
+    far_of_pair = (1 - rank // 2) * 2 + (1 - rank % 2)
+    for piece in range(pieces):
+        pair_out[0, piece] = product(far_of_pair, piece).astype(jnp.bfloat16)
+        to_pair(0, piece).start()
+        mine = product(far, piece)
+        to_pair(0, piece).wait_recv()
+        far_out[piece] = (mine + pair_in[0, piece].astype(jnp.float32)).astype(jnp.bfloat16)
+        to_far(piece).start()
+    for piece in range(pieces):
+        pair_out[1, piece] = product(pair, piece).astype(jnp.bfloat16)
+        to_pair(1, piece).start()
+        mine = product(rank, piece)
+        to_pair(1, piece).wait_recv()
+        kept[piece] = mine + pair_in[1, piece].astype(jnp.float32)
+    for piece in range(pieces):
+        to_far(piece).wait_recv()
+        out_ref[:, piece * tile:(piece + 1) * tile] = (
+            kept[piece] + far_in[piece].astype(jnp.float32)
+        ).astype(out_ref.dtype)
+
+    for chunk in range(chunks):
+        for mask in masks:
+            exchange(*there, chunk, mask).wait_send()
+            exchange(*back, chunk, mask).wait_send()
+    for piece in range(pieces):
+        for side in range(2):
+            to_pair(side, piece).wait_send()
+        to_far(piece).wait_send()
+
+
+def local_fused(projections, routes, segments, out_weight):
+    senders = lax.axis_size("dp")
+    ranks = lax.axis_size("tensor")
+    own_rows, _, columns = projections.shape
+    positions = segments.shape[1]
+    capacity = positions // senders
+    width_out = out_weight.shape[1]
+    block = width_out // ranks
+    heads_step = 2 if (columns // HD) % 2 == 0 else 1
+    width = heads_step * HD
+    chunks = columns // width
+    pieces = block // 512
+    slot_of_row, group_ids = routing(routes, segments, own_rows, senders, capacity)
+    bf16, f32 = jnp.bfloat16, jnp.float32
+    vmem = pl.BlockSpec(memory_space=pltpu.VMEM)
+    return pl.pallas_call(
+        functools.partial(fused_kernel, senders, heads_step),
+        out_shape=jax.ShapeDtypeStruct((own_rows, block), bf16),
+        in_specs=[vmem] * 5 + [pl.BlockSpec(memory_space=pl.ANY)],
+        out_specs=vmem,
+        scratch_shapes=[
+            pltpu.VMEM((columns, width_out), bf16),
+            pltpu.VMEM((chunks, positions, 3 * width), bf16),
+            pltpu.VMEM((chunks, positions, 3 * width), bf16),
+            pltpu.VMEM((chunks, positions, width), bf16),
+            pltpu.VMEM((chunks, positions, width), bf16),
+            pltpu.VMEM((own_rows, columns), bf16),
+            pltpu.VMEM((2, pieces, own_rows, 512), bf16),
+            pltpu.VMEM((2, pieces, own_rows, 512), bf16),
+            pltpu.VMEM((pieces, own_rows, 512), bf16),
+            pltpu.VMEM((pieces, own_rows, 512), bf16),
+            pltpu.VMEM((pieces, own_rows, 512), f32),
+            pltpu.SemaphoreType.DMA(()),
+            pltpu.SemaphoreType.DMA((chunks, senders)),
+            pltpu.SemaphoreType.DMA((chunks, senders)),
+            pltpu.SemaphoreType.DMA((chunks, senders)),
+            pltpu.SemaphoreType.DMA((chunks, senders)),
+            pltpu.SemaphoreType.DMA((2, pieces)),
+            pltpu.SemaphoreType.DMA((2, pieces)),
+            pltpu.SemaphoreType.DMA((pieces,)),
+            pltpu.SemaphoreType.DMA((pieces,)),
+        ],
+        compiler_params=pltpu.CompilerParams(
+            collective_id=0, has_side_effects=True, vmem_limit_bytes=50 * 2**20
+        ),
+    )(
+        slot_of_row[None, :], slot_of_row[:, None], group_ids[None, :], group_ids[:, None],
+        jnp.transpose(projections, (1, 0, 2)), out_weight,
+    )
+
+
 def solution(mesh):
     in_specs = (P("dp", None, "tensor"), P(), P("dp", None), P("tensor", None))
     out_specs = P("dp", "tensor")
-    return jax.shard_map(local, mesh=mesh, in_specs=in_specs, out_specs=out_specs, check_vma=False)
+    senders, ranks = mesh.shape["dp"], mesh.shape["tensor"]
+
+    def program(projections, routes, segments, out_weight):
+        capacity = segments.shape[1] // senders
+        fused = (
+            ranks == 4
+            and senders & (senders - 1) == 0
+            and capacity % 16 == 0
+            and (out_weight.shape[1] // ranks) % 512 == 0
+        )
+        body = jax.shard_map(
+            local_fused if fused else local, mesh=mesh, in_specs=in_specs, out_specs=out_specs, check_vma=False
+        )
+        return body(projections, routes, segments, out_weight)
+
+    return program

time: 192 us -> 111 us (0.58)
  waiting for transfers between devices: 120 us -> 0 us
  Pallas kernels: 0 us -> 104 us
  local copies, waits for them, and re-layouts: 30.7 us -> 3.9 us
  between operations: 13.5 us -> 0.07 us
  matrix products: 11.7 us -> 0 us
  starting transfers between devices: 11.1 us -> 0 us
  other arithmetic: 4.85 us -> 2.57 us
    pallas_call x0 -> x1, Pallas kernels: none -> 104 us  [local_fused(): pl.pallas_call(functools.partial(fused_kernel, senders, heads_step), out_...]
    all_to_all x2 -> x0, waiting for transfers between devices: 73 us -> none  [the longest x1 52.9 us: local(): lax.all_to_all(outgoing, 'dp', split_axis=0, concat_axis=0, tiled=True)]
    reduce_scatter x1 -> x0, waiting for transfers between devices: 47 us -> none  [local(): lax.psum_scatter(partial_value.astype(jnp.bfloat16), 'tensor', scatter_di...]
    dot_general x3 -> x0, matrix products: 11.7 us -> none  [the longest x1 9.13 us: local(): partial_value = jnp.dot(own, out_weight, preferred_element_type=jnp.float32)]
    gather x2 -> x0, local copies, waits for them, and re-layouts: 11.2 us -> none  [the longest x1 9.03 us: local(): projections[source_row].reshape(senders, capacity, 3, heads_here, HD)]
    all_to_all x2 -> x0, starting transfers between devices: 10.9 us -> none  [the longest x1 7.25 us: local(): lax.all_to_all(outgoing, 'dp', split_axis=0, concat_axis=0, tiled=True)]
    reshape x2 -> x0, local copies, waits for them, and re-layouts: 10 us -> none  [local(): projections[source_row].reshape(senders, capacity, 3, heads_here, HD)]
    sub x1 -> x0, other arithmetic: 3 us -> none  [one_block(): raised = jnp.exp(scores - jnp.max(scores, axis=2, keepdims=True))]
  transfers between devices with their start and end apart: 3 -> 0, of which waited for: 3 -> 0; matrix products, arithmetic and copies ran while one was open for 1% -> 0% of each run, Pallas kernels for 0% -> 0%
where the time goes in v2:
time: 111 us
  Pallas kernels  104 us (94%)
  local copies, waits for them, and re-layouts  3.9 us (4%)
  other arithmetic  2.57 us (2%)
    pallas_call x1, Pallas kernels, local_fused(): pl.pallas_call(functools.partial(fused_kernel, senders, heads_step), out_...  104 us
    unnamed x4, local copies, waits for them, and re-layouts  2.63 us

profile of v2, /device:TPU:0, one launch (start us, length us, event | category | flops | bytes accessed | tf_op | source)
XLA Modules:
  0.0 110.9 jit_solution(6607639445446262840)
XLA Ops:
  0.0 0.7 fusion.2
  0.7 0.2 convert_reduce_fusion
  0.9 0.8 fusion.1
  1.7 0.1 reduce_sum.47
  1.8 0.1 select_reduce_fusion.1
  1.9 0.1 iota_compare_fusion.3
  2.0 0.1 lt.72
  2.1 0.1 iota_add_fusion
  2.2 0.1 add.39
  2.2 0.9 select_reduce_fusion
  3.2 0.3 lt.78
  3.5 0.1 copy.14
  3.6 0.2 reshape_add_fusion
  3.8 0.1 copy.13
  4.0 0.0 copy-start
  4.0 1.5 %copy-done = bf16[384,3,768]{2,0,1:T(8,128)(2,1)S(1)} copy-done((bf16[384,3,768]{2,0,1:T(8,128)(2,1)S(1)}, bf16[384,3,768]{2,0,1:T(8,128)(2,1)}, u32[]{:S(2)}) %copy-start) | copy-done | bytes 1769496
  5.5 104.3 %shard_map.46 = bf16[384,1536]{1,0:T(8,128)(2,1)S(1)} custom-call(s32[1,384]{1,0:T(1,128)S(1)} %reshape_add_fusion.1.slot_row_ref, s32[384,1]{1,0:T(8,128)S(1)} %get-tuple-element.7.slot_col_ref, s32[1,512]{1,0:T(1,128)S(1)} %subtract_select_fusion.1.ids_row_ref, s32[512,1]{1,0:T(8,128)S(1)} %subtract_select_fusion.ids_col_ref, ...), custom_call_target="tpu_custom_call" | custom-call | tf_op jit(solution)/shard_map/pallas_call | solution.py:249
  109.8 1.0 copy.17
  (4 shorter events, 0.1 us)
Async XLA Ops:
  4.0 1.5 %copy-start = (bf16[384,3,768]{2,0,1:T(8,128)(2,1)S(1)}, bf16[384,3,768]{2,0,1:T(8,128)(2,1)}, u32[]{:S(2)}) copy-start(bf16[384,3,768]{2,0,1:T(8,128)(2,1)} %param.4) | copy-start | bytes 5308420

commit v3 on v1

--- a/solution.py
+++ b/solution.py
@@ -9,6 +9,7 @@
 from jax.sharding import PartitionSpec as P
 
 HD = 128
+SPLITS = 4
 
 
 def routing(routes, segments, own_rows, senders, capacity):
@@ -69,7 +70,264 @@
     return lax.psum_scatter(partial_value.astype(jnp.bfloat16), "tensor", scatter_dimension=1, tiled=True)
 
 
+def xor(index, mask, size):
+    result, bit = 0, 1
+    while bit < size:
+        digit = (index // bit) % 2
+        result = result + ((1 - digit) if (mask // bit) % 2 else digit) * bit
+        bit *= 2
+    return result
+
+
+def fused_kernel(
+    senders, splits, heads_step,
+    slot_row_ref, turn_row_ref, turn_col_ref, ids_row_ref, ids_col_ref, proj_ref, weight_hbm,
+    out_ref,
+    weight, packed_q, arrived_q, packed_kv, arrived_kv, attended, returned,
+    pair_out, pair_in, far_out, far_in, kept, summed,
+    weight_sem, q_send, q_recv, kv_send, kv_recv, back_send, back_recv, pair_send, pair_recv, far_send, far_recv,
+):
+    own_rows, columns = proj_ref.shape[1], proj_ref.shape[2]
+    chunks, positions, _ = packed_kv.shape
+    capacity = positions // senders
+    sub = capacity // splits
+    rows = senders * sub
+    width = heads_step * HD
+    block = out_ref.shape[1]
+    me = lax.axis_index("dp")
+    rank = lax.axis_index("tensor")
+    pair = (rank // 2) * 2 + (1 - rank % 2)
+    far = (1 - rank // 2) * 2 + rank % 2
+    far_of_pair = (1 - rank // 2) * 2 + (1 - rank % 2)
+    masks = list(range(senders // 2, senders)) + list(range(senders // 2 - 1, 0, -1))
+    f32, bf16 = jnp.float32, jnp.bfloat16
+
+    fetch = pltpu.make_async_copy(weight_hbm, weight, weight_sem)
+    fetch.start()
+    barrier = pltpu.get_barrier_semaphore()
+    for mask in masks:
+        pl.semaphore_signal(barrier, inc=1, device_id=(xor(me, mask, senders), rank), device_id_type=pl.DeviceIdType.MESH)
+    for other in (pair, far):
+        pl.semaphore_signal(barrier, inc=1, device_id=(me, other), device_id_type=pl.DeviceIdType.MESH)
+    pl.semaphore_wait(barrier, len(masks) + 2)
+
+    def rows_of(device, size):
+        return pl.ds(pl.multiple_of(device * size, size), size)
+
+    def copy(kind, at, mask, arriving=False):
+        source, target, send_sem, recv_sem, size = kind
+        peer = xor(me, mask, senders)
+        first, second = (me, peer) if arriving else (peer, me)
+        return pltpu.make_async_remote_copy(
+            src_ref=source.at[at, rows_of(first, size)],
+            dst_ref=target.at[at, rows_of(second, size)],
+            send_sem=send_sem.at[at, mask],
+            recv_sem=recv_sem.at[at, mask],
+            device_id=(peer, rank),
+            device_id_type=pl.DeviceIdType.MESH,
+        )
+
+    def send(kind, at):
+        source, target, _, _, size = kind
+        for mask in masks:
+            copy(kind, at, mask).start()
+        target[at, rows_of(me, size)] = source[at, rows_of(me, size)]
+
+    def receive(kind, at):
+        for mask in masks:
+            copy(kind, at, mask, arriving=True).wait_recv()
+
+    queries = (packed_q, arrived_q, q_send, q_recv, sub)
+    pairs = (packed_kv, arrived_kv, kv_send, kv_recv, capacity)
+    back = (attended, returned, back_send, back_recv, sub)
+
+    def one_hot(count, targets):
+        hits = lax.broadcasted_iota(jnp.int32, (count, own_rows), 0) == targets
+        return hits.astype(f32).astype(bf16)
+
+    def pick(matrix, piece):
+        return jnp.dot(matrix, piece, preferred_element_type=f32).astype(bf16)
+
+    def pack_queries(split):
+        packed_q[split] = pick(one_hot(rows, turn_row_ref[...] - split * rows), proj_ref[0])
+
+    pack_queries(0)
+    send(queries, 0)
+    place = one_hot(positions, slot_row_ref[...])
+    for chunk in range(chunks):
+        for part in range(2):
+            packed_kv[chunk, :, part * width:(part + 1) * width] = pick(
+                place, proj_ref[1 + part, :, chunk * width:(chunk + 1) * width]
+            )
+        send(pairs, chunk)
+    for split in range(1, splits):
+        pack_queries(split)
+    ahead = min(2, splits)
+    for split in range(1, ahead):
+        send(queries, split)
+
+    scale = 1.0 / math.sqrt(HD)
+
+    def attend(split):
+        receive(queries, split)
+        allowed = ids_col_ref[split * rows:(split + 1) * rows] == ids_row_ref[...]
+        for chunk in range(chunks):
+            if split == 0:
+                receive(pairs, chunk)
+            for head in range(heads_step):
+                at = head * HD
+                column = chunk * width + at
+                query = arrived_q[split, :, column:column + HD]
+                key = arrived_kv[chunk, :, at:at + HD]
+                value = arrived_kv[chunk, :, width + at:width + at + HD]
+                scores = lax.dot_general(query, key, (((1,), (1,)), ((), ())), preferred_element_type=f32) * scale
+                scores = jnp.where(allowed, scores, -jnp.inf)
+                raised = jnp.exp(scores - jnp.max(scores, axis=1, keepdims=True))
+                weights = (raised / jnp.sum(raised, axis=1, keepdims=True)).astype(bf16)
+                attended[split, :, column:column + HD] = pick(weights, value)
+        send(back, split)
+        if split + ahead < splits:
+            send(queries, split + ahead)
+
+    def product(split, target):
+        start = pl.multiple_of(target * block, block)
+        return jnp.dot(returned[split], weight[:, pl.ds(start, block)], preferred_element_type=f32)
+
+    def to_pair(side, split):
+        return pltpu.make_async_remote_copy(
+            src_ref=pair_out.at[side, split],
+            dst_ref=pair_in.at[side, split],
+            send_sem=pair_send.at[side, split],
+            recv_sem=pair_recv.at[side, split],
+            device_id=(me, pair),
+            device_id_type=pl.DeviceIdType.MESH,
+        )
+
+    def to_far(split):
+        return pltpu.make_async_remote_copy(
+            src_ref=far_out.at[split],
+            dst_ref=far_in.at[split],
+            send_sem=far_send.at[split],
+            recv_sem=far_recv.at[split],
+            device_id=(me, far),
+            device_id_type=pl.DeviceIdType.MESH,
+        )
+
+    def project(split):
+        receive(back, split)
+        if split == 0:
+            fetch.wait()
+        pair_out[0, split] = product(split, far_of_pair).astype(bf16)
+        to_pair(0, split).start()
+        mine = product(split, far)
+        to_pair(0, split).wait_recv()
+        far_out[split] = (mine + pair_in[0, split].astype(f32)).astype(bf16)
+        to_far(split).start()
+        pair_out[1, split] = product(split, pair).astype(bf16)
+        to_pair(1, split).start()
+        kept[split] = product(split, rank)
+
+    for split in range(splits):
+        attend(split)
+        if split >= 1:
+            project(split - 1)
+    project(splits - 1)
+    for split in range(splits):
+        to_pair(1, split).wait_recv()
+        total = kept[split] + pair_in[1, split].astype(f32)
+        to_far(split).wait_recv()
+        summed[split * rows:(split + 1) * rows] = (total + far_in[split].astype(f32)).astype(bf16)
+    unplace = turn_col_ref[...] == lax.broadcasted_iota(jnp.int32, (own_rows, positions), 1)
+    out_ref[...] = pick(unplace.astype(f32).astype(bf16), summed[...])
+
+    for mask in masks:
+        for chunk in range(chunks):
+            copy(pairs, chunk, mask).wait_send()
+        for split in range(splits):
+            copy(queries, split, mask).wait_send()
+            copy(back, split, mask).wait_send()
+    for split in range(splits):
+        to_pair(0, split).wait_send()
+        to_pair(1, split).wait_send()
+        to_far(split).wait_send()
+
+
+def local_fused(projections, routes, segments, out_weight):
+    senders = lax.axis_size("dp")
+    ranks = lax.axis_size("tensor")
+    own_rows, _, columns = projections.shape
+    positions = segments.shape[1]
+    capacity = positions // senders
+    width_out = out_weight.shape[1]
+    block = width_out // ranks
+    heads_step = 2 if (columns // HD) % 2 == 0 else 1
+    width = heads_step * HD
+    chunks = columns // width
+    splits = SPLITS if capacity % (16 * SPLITS) == 0 else 1
+    sub = capacity // splits
+    rows = senders * sub
+    slot_of_row, group_ids = routing(routes, segments, own_rows, senders, capacity)
+    turn = ((slot_of_row % capacity) // sub) * rows + (slot_of_row // capacity) * sub + slot_of_row % sub
+    ids_turned = group_ids.reshape(senders, splits, sub).transpose(1, 0, 2).reshape(positions, 1)
+    bf16, f32 = jnp.bfloat16, jnp.float32
+    vmem = pl.BlockSpec(memory_space=pltpu.VMEM)
+    dma = pltpu.SemaphoreType.DMA
+    return pl.pallas_call(
+        functools.partial(fused_kernel, senders, splits, heads_step),
+        out_shape=jax.ShapeDtypeStruct((own_rows, block), bf16),
+        in_specs=[vmem] * 6 + [pl.BlockSpec(memory_space=pl.ANY)],
+        out_specs=vmem,
+        scratch_shapes=[
+            pltpu.VMEM((columns, width_out), bf16),
+            pltpu.VMEM((splits, rows, columns), bf16),
+            pltpu.VMEM((splits, rows, columns), bf16),
+            pltpu.VMEM((chunks, positions, 2 * width), bf16),
+            pltpu.VMEM((chunks, positions, 2 * width), bf16),
+            pltpu.VMEM((splits, rows, columns), bf16),
+            pltpu.VMEM((splits, rows, columns), bf16),
+            pltpu.VMEM((2, splits, rows, block), bf16),
+            pltpu.VMEM((2, splits, rows, block), bf16),
+            pltpu.VMEM((splits, rows, block), bf16),
+            pltpu.VMEM((splits, rows, block), bf16),
+            pltpu.VMEM((splits, rows, block), f32),
+            pltpu.VMEM((positions, block), bf16),
+            dma(()),
+            dma((splits, senders)),
+            dma((splits, senders)),
+            dma((chunks, senders)),
+            dma((chunks, senders)),
+            dma((splits, senders)),
+            dma((splits, senders)),
+            dma((2, splits)),
+            dma((2, splits)),
+            dma((splits,)),
+            dma((splits,)),
+        ],
+        compiler_params=pltpu.CompilerParams(
+            collective_id=0, has_side_effects=True, vmem_limit_bytes=50 * 2**20
+        ),
+    )(
+        slot_of_row[None, :], turn[None, :], turn[:, None], group_ids[None, :], ids_turned,
+        jnp.transpose(projections, (1, 0, 2)), out_weight,
+    )
+
+
 def solution(mesh):
     in_specs = (P("dp", None, "tensor"), P(), P("dp", None), P("tensor", None))
     out_specs = P("dp", "tensor")
-    return jax.shard_map(local, mesh=mesh, in_specs=in_specs, out_specs=out_specs, check_vma=False)
+    senders, ranks = mesh.shape["dp"], mesh.shape["tensor"]
+
+    def program(projections, routes, segments, out_weight):
+        capacity = segments.shape[1] // senders
+        fused = (
+            ranks == 4
+            and senders & (senders - 1) == 0
+            and capacity % 16 == 0
+            and (out_weight.shape[1] // ranks) % 512 == 0
+        )
+        body = jax.shard_map(
+            local_fused if fused else local, mesh=mesh, in_specs=in_specs, out_specs=out_specs, check_vma=False
+        )
+        return body(projections, routes, segments, out_weight)
+
+    return program

time: 192 us -> 106 us (0.55)
  waiting for transfers between devices: 120 us -> 0 us
  Pallas kernels: 0 us -> 98.2 us
  local copies, waits for them, and re-layouts: 30.7 us -> 3.74 us
  between operations: 13.5 us -> 0.07 us
  matrix products: 11.7 us -> 0 us
  starting transfers between devices: 11.1 us -> 0 us
  other arithmetic: 4.85 us -> 2.92 us
    pallas_call x0 -> x1, Pallas kernels: none -> 98.2 us  [local_fused(): pl.pallas_call(functools.partial(fused_kernel, senders, splits, heads_ste...]
    all_to_all x2 -> x0, waiting for transfers between devices: 73 us -> none  [the longest x1 52.9 us: local(): lax.all_to_all(outgoing, 'dp', split_axis=0, concat_axis=0, tiled=True)]
    reduce_scatter x1 -> x0, waiting for transfers between devices: 47 us -> none  [local(): lax.psum_scatter(partial_value.astype(jnp.bfloat16), 'tensor', scatter_di...]
    dot_general x3 -> x0, matrix products: 11.7 us -> none  [the longest x1 9.13 us: local(): partial_value = jnp.dot(own, out_weight, preferred_element_type=jnp.float32)]
    gather x2 -> x0, local copies, waits for them, and re-layouts: 11.2 us -> none  [the longest x1 9.03 us: local(): projections[source_row].reshape(senders, capacity, 3, heads_here, HD)]
    all_to_all x2 -> x0, starting transfers between devices: 10.9 us -> none  [the longest x1 7.25 us: local(): lax.all_to_all(outgoing, 'dp', split_axis=0, concat_axis=0, tiled=True)]
    reshape x2 -> x1, local copies, waits for them, and re-layouts: 10 us -> 0.16 us  [local_fused(): group_ids.reshape(senders, splits, sub).transpose(1, 0, 2)]
    sub x1 -> x0, other arithmetic: 3 us -> none  [one_block(): raised = jnp.exp(scores - jnp.max(scores, axis=2, keepdims=True))]
  transfers between devices with their start and end apart: 3 -> 0, of which waited for: 3 -> 0; matrix products, arithmetic and copies ran while one was open for 1% -> 0% of each run, Pallas kernels for 0% -> 0%
where the time goes in v3:
time: 106 us; the launch traced here: 105 us
  Pallas kernels  98.2 us (93%)
  local copies, waits for them, and re-layouts  3.74 us (4%)
  other arithmetic  2.92 us (3%)
    pallas_call x1, Pallas kernels, local_fused(): pl.pallas_call(functools.partial(fused_kernel, senders, splits, heads_ste...  98.2 us
    unnamed x4, local copies, waits for them, and re-layouts  2.62 us

profile of v3, /device:TPU:0, one launch (start us, length us, event | category | flops | bytes accessed | tf_op | source)
XLA Modules:
  0.0 104.9 jit_solution(7649295342969670111)
XLA Ops:
  0.0 0.7 fusion.12
  0.7 0.2 convert_reduce_fusion
  0.9 0.8 fusion.10
  1.7 0.1 reduce_sum.47
  1.8 0.1 select_reduce_fusion.1
  1.9 0.1 iota_compare_fusion.3
  2.0 0.1 lt.93
  2.1 0.1 iota_add_fusion
  2.2 0.1 add.131
  2.3 0.9 select_reduce_fusion
  3.2 0.1 reduce_sum.51
  3.3 0.1 select_bitcast_fusion
  3.4 0.1 copy.14
  3.5 0.5 fusion.4
  4.1 0.2 reshape.257.ids_col_ref
  4.2 0.0 copy-start
  4.2 1.5 %copy-done = bf16[384,3,768]{2,0,1:T(8,128)(2,1)S(1)} copy-done((bf16[384,3,768]{2,0,1:T(8,128)(2,1)S(1)}, bf16[384,3,768]{2,0,1:T(8,128)(2,1)}, u32[]{:S(2)}) %copy-start) | copy-done | bytes 1769496
  5.7 98.2 %shard_map.46 = bf16[384,1536]{1,0:T(8,128)(2,1)S(1)} custom-call(s32[1,384]{1,0:T(1,128)S(1)} %get-tuple-element.6.slot_row_ref, s32[1,384]{1,0:T(1,128)S(1)} %get-tuple-element.5.turn_row_ref, s32[384,1]{1,0:T(8,128)S(1)} %get-tuple-element.9.turn_col_ref, s32[1,512]{1,0:T(1,128)S(1)} %subtract_select_fusion.ids_row_ref, ...), custom_call_target="tpu_custom_call" | custom-call | tf_op jit(solution)/shard_map/pallas_call | solution.py:275
  103.9 1.0 copy.17
  (5 shorter events, 0.1 us)
Async XLA Ops:
  4.2 1.5 %copy-start = (bf16[384,3,768]{2,0,1:T(8,128)(2,1)S(1)}, bf16[384,3,768]{2,0,1:T(8,128)(2,1)}, u32[]{:S(2)}) copy-start(bf16[384,3,768]{2,0,1:T(8,128)(2,1)} %param.4) | copy-start | bytes 5308420
